TPU v7x, 512 devices: a whole 4x8x8 slice. The times are simulated.
512 devices in a mesh: section: 8 (over z), expert: 32 (over y, x), dp: 2 (over core).
Axes of the slice: x: 4, y: 8, z: 8, core: 2. Of those that a mesh axis runs over, the one named last changes fastest.
Arguments:
- blocks: bfloat16 [8, 8192, 3072], P('section', ('dp', 'expert')), parts along dimension 1, may hold values from -6 to 6
- norm_gain: bfloat16 [8, 3072], P('section'), may hold values from 0.25 to 1.75
- w_gate: bfloat16 [8, 3072, 6144], P('section', None, 'expert'), may hold values from -0.109375 to 0.109375
- w_up: bfloat16 [8, 3072, 6144], P('section', None, 'expert'), may hold values from -0.109375 to 0.109375
- w_down: bfloat16 [8, 6144, 3072], P('section', 'expert'), may hold values from -0.15625 to 0.15625
- route_ids: int32 [8, 8192, 2], P('section', ('dp', 'expert')), parts along dimension 1, may hold values from 0 to 11, as said below
- route_weights: float32 [8, 8192, 2], P('section', ('dp', 'expert')), parts along dimension 1, may hold values from 0.05 to 1
Outputs:
- mixed: bfloat16 [8, 8192, 3072], P('section', ('dp', 'expert')), parts along dimension 1
There are 2 independent parts, one for each index of `dp`. A program takes and returns all parts, laid end to end along the dimension named above; an argument that names none is the same for every part. Nothing has to cross between parts.
Inputs may be any that keep to these rules, and one draw needn't show every extreme that they name: `route_ids`: each token names 2 different ids. Within each aligned block of 128 tokens of a section (the tokens of one device), every computing expert (ids below 4) is named exactly 32 times and every zero-computation id at most 32 times.
All inputs are finite; a program needn't handle non-finite values.
Results may differ from a plain program's by a relative error of at most 0.0085.
Values may be sent and summed in bfloat16 or wider, within the bound.
A program may use at most 64 MiB of HBM per device.

v0:
```python
import jax
import jax.numpy as jnp
from jax import lax
from jax.sharding import PartitionSpec as P

HID = 1536
CAP = 32


def passed_along(value, axis, steps):
    count = lax.axis_size(axis)
    pairs = [(source, (source + steps) % count) for source in range(count)]
    return lax.ppermute(value, axis, pairs)


def local(blocks, norm_gain, w_gate, w_up, w_down, route_ids, route_weights):
    arrived = passed_along(blocks, "section", 1)[0]
    residual = arrived.astype(jnp.float32)
    inverse = lax.rsqrt(jnp.mean(residual * residual, axis=-1, keepdims=True) + 1e-06)
    normed = (residual * inverse * norm_gain[0].astype(jnp.float32)).astype(jnp.bfloat16)
    slice_width = w_gate.shape[2]
    slice_count = HID // slice_width
    experts = lax.axis_size("expert") // slice_count
    token_count = arrived.shape[0]
    pick_count = route_ids.shape[2]
    pick_ids = route_ids[0].reshape(-1)
    member = (pick_ids[:, None] == jnp.arange(experts, dtype=jnp.int32)[None, :]).astype(jnp.int32)
    slot_rank = jnp.cumsum(member, axis=0) - 1
    slot_range = jnp.arange(CAP, dtype=jnp.int32)
    slot_table = (member[:, :, None] == 1) & (slot_rank[:, :, None] == slot_range[None, None, :])
    slot_table = slot_table.astype(jnp.float32).reshape(token_count, pick_count, experts, CAP)
    dispatch_table = jnp.sum(slot_table, axis=1)
    weighted_table = jnp.einsum(
        "tjec,tj->tec", slot_table, route_weights[0], precision=lax.Precision.HIGHEST
    )
    buffer = jnp.einsum(
        "tec,td->ecd",
        dispatch_table.astype(jnp.bfloat16),
        normed,
        preferred_element_type=jnp.float32,
    ).astype(jnp.bfloat16)
    outgoing = jnp.repeat(buffer, slice_count, axis=0)
    received = lax.all_to_all(outgoing, "expert", split_axis=0, concat_axis=0, tiled=True)
    flat_rows = received.reshape(-1, received.shape[-1])
    gate_act = jnp.dot(flat_rows, w_gate[0], preferred_element_type=jnp.float32)
    up_act = jnp.dot(flat_rows, w_up[0], preferred_element_type=jnp.float32)
    hidden = (jax.nn.silu(gate_act) * up_act).astype(jnp.bfloat16)
    partial_value = jnp.dot(hidden, w_down[0], preferred_element_type=jnp.float32).astype(
        jnp.bfloat16
    )
    returned = lax.all_to_all(
        partial_value.reshape(received.shape), "expert", split_axis=0, concat_axis=0, tiled=True
    )
    expert_out = jnp.sum(
        returned.reshape(experts, slice_count, CAP, returned.shape[-1]).astype(jnp.float32), axis=1
    )
    zero_weight = jnp.sum(jnp.where(route_ids[0] >= experts, route_weights[0], 0.0), axis=1)
    mixed = residual + zero_weight[:, None] * normed.astype(jnp.float32)
    mixed = mixed + jnp.einsum(
        "tec,ecd->td", weighted_table, expert_out, precision=lax.Precision.HIGHEST
    )
    return mixed.astype(jnp.bfloat16)[None]


def solution(mesh):
    placed = (
        P("section", ("dp", "expert"), None),
        P("section", None),
        P("section", None, "expert"),
        P("section", None, "expert"),
        P("section", "expert", None),
        P("section", ("dp", "expert"), None),
        P("section", ("dp", "expert"), None),
    )
    return jax.shard_map(
        local,
        mesh=mesh,
        in_specs=placed,
        out_specs=P("section", ("dp", "expert"), None),
        check_vma=False,
    )
```

profile of v0, /device:TPU:1, one launch (start us, length us, event | category | flops | bytes accessed | tf_op | source)
XLA Modules:
  0.0 344.9 jit_solution(8835517618149976118)
XLA Ops:
  0.0 0.0 copy-start
  0.0 4.9 %collective-permute-start = (bf16[1,128,3072]{2,1,0:T(8,128)(2,1)}, bf16[1,128,3072]{2,1,0:T(8,128)(2,1)S(1)}, u32[]{:S(2)}, u32[]{:S(2)}) collective-permute-start(bf16[1,128,3072]{2,1,0:T(8,128)(2,1)} %param.7), channel_id=1, source_target_pairs={{0,64},{64,128},{128,192},{192,256},{256,320},{320,384},{384,448},... | collective-permute-start | bytes 2359304 | tf_op jit(solution)/shard_map/ppermute | solution.py:13
  5.0 0.8 copy.17
  5.7 0.1 eq.60
  5.9 1.2 reduce-window.6
  7.1 0.1 slice.8
  7.2 0.1 copy.18
  7.3 0.1 copy.19
  7.4 0.1 add_add_fusion
  7.5 0.1 copy.26
  7.7 0.1 copy.21
  7.7 0.7 mul.50
  8.5 0.7 convert_compare_fusion
  9.2 0.7 convert_reduce_fusion.1
  9.9 19.2 %collective-permute-done = bf16[1,128,3072]{2,1,0:T(8,128)(2,1)S(1)} collective-permute-done((bf16[1,128,3072]{2,1,0:T(8,128)(2,1)}, bf16[1,128,3072]{2,1,0:T(8,128)(2,1)S(1)}, u32[]{:S(2)}, u32[]{:S(2)}) %collective-permute-start) | collective-permute-done | bytes 786464 | tf_op jit(solution)/shard_map/ppermute | solution.py:13
  29.1 0.2 fusion
  29.3 0.5 convolution_convert_fusion.1
  29.8 0.8 broadcast_in_dim.9
  30.6 0.0 copy-start.4
  30.6 147.6 %all_to_all.10 = bf16[32,32,3072]{2,1,0:T(8,128)(2,1)S(1)} all-to-all(bf16[32,32,3072]{2,1,0:T(8,128)(2,1)S(1)} %bitcast.51), channel_id=1, replica_groups=mesh['section'=8,'expert'=32,'dp'=2] {'expert'}, dimensions={0} | all-to-all | bytes 12582912 | tf_op jit(solution)/shard_map/all_to_all | solution.py:43
  178.2 0.0 copy-start.1
  178.2 2.7 copy-done.1
  180.9 0.0 copy-done.4
  180.9 0.0 copy-start.5
  180.9 3.1 fusion.9
  184.0 0.0 copy-done
  184.0 0.0 copy-done.5
  184.0 11.0 %convolution_convert_fusion = bf16[1024,3072]{1,0:T(8,128)(2,1)} fusion(bf16[1024,3072]{1,0:T(8,128)(2,1)} %bitcast.54, bf16[1,192,3072]{2,1,0:T(8,128)(2,1)S(1)} %copy-done, bf16[1,3072,192]{1,2,0:T(8,128)(2,1)S(1)} %copy-done.5, f32[1024,192]{0,1:T(8,128)} %fusion.9), kind=kOutput, calls=%fused_computation.1 | convolution fusion | flops 2420244480 | bytes 15728640 | tf_op jit(solution)/shard_map/dot_general | solution.py:48
  195.0 0.0 copy-start.2
  195.0 0.0 copy-start.3
  195.0 6.9 %all-to-all-start.1 = ((bf16[32,32,3072]{2,1,0:T(8,128)(2,1)}), bf16[32,32,3072]{2,1,0:T(8,128)(2,1)}, u32[]{:S(2)}, u32[]{:S(2)}) async-start(bf16[32,32,3072]{2,1,0:T(8,128)(2,1)} %bitcast.52), calls=%async_computation.1 | async-start | bytes 12582912 | tf_op jit(solution)/shard_map/all_to_all | solution.py:51
  201.9 0.0 copy-done.2
  201.9 0.0 copy-done.3
  202.0 136.3 %all-to-all-done.1 = bf16[32,32,3072]{2,1,0:T(8,128)(2,1)} async-done(((bf16[32,32,3072]{2,1,0:T(8,128)(2,1)}), bf16[32,32,3072]{2,1,0:T(8,128)(2,1)}, u32[]{:S(2)}, u32[]{:S(2)}) %all-to-all-start.1) | async-done | bytes 6291488 | tf_op jit(solution)/shard_map/all_to_all | solution.py:51
  338.3 4.0 %convert_reduce_fusion = f32[4,32,3072]{2,1,0:T(8,128)S(1)} fusion(bf16[32,32,3072]{2,1,0:T(8,128)(2,1)} %all-to-all-done.1), kind=kLoop, calls=%fused_computation | loop fusion | flops 5898240 | bytes 7864320 | tf_op jit(solution)/shard_map/reduce_sum | solution.py:54
  342.3 2.6 fusion.11
  (5 shorter events, 0.1 us)
Async XLA Ops:
  0.0 184.0 %copy-start = (bf16[1,192,3072]{2,1,0:T(8,128)(2,1)S(1)}, bf16[1,192,3072]{2,1,0:T(8,128)(2,1)}, u32[]{:S(2)}) copy-start(bf16[1,192,3072]{2,1,0:T(8,128)(2,1)} %param.11) | copy-start | bytes 3538948
  0.0 29.1 %collective-permute-start = (bf16[1,128,3072]{2,1,0:T(8,128)(2,1)}, bf16[1,128,3072]{2,1,0:T(8,128)(2,1)S(1)}, u32[]{:S(2)}, u32[]{:S(2)}) collective-permute-start(bf16[1,128,3072]{2,1,0:T(8,128)(2,1)} %param.7), channel_id=1, source_target_pairs={{0,64},{64,128},{128,192},{192,256},{256,320},{320,384},{384,448},... | collective-permute-start | bytes 2359304 | tf_op jit(solution)/shard_map/ppermute | solution.py:13
  30.6 150.3 %copy-start.4 = (bf16[1,3072,192]{1,2,0:T(8,128)(2,1)S(1)}, bf16[1,3072,192]{1,2,0:T(8,128)(2,1)}, u32[]{:S(2)}) copy-start(bf16[1,3072,192]{1,2,0:T(8,128)(2,1)} %param.9) | copy-start | bytes 3538948
  178.2 2.7 copy-start.1
  180.9 3.1 copy-start.5
  195.0 6.9 %copy-start.2 = (s32[1,128,2]{1,2,0:T(2,128)S(1)}, s32[1,128,2]{1,2,0:T(2,128)}, u32[]{:S(2)}) copy-start(s32[1,128,2]{1,2,0:T(2,128)} %param.12) | copy-start | bytes 3076
  195.0 6.9 %copy-start.3 = (f32[1,128,2]{1,2,0:T(2,128)S(1)}, f32[1,128,2]{1,2,0:T(2,128)}, u32[]{:S(2)}) copy-start(f32[1,128,2]{1,2,0:T(2,128)} %param.13) | copy-start | bytes 3076
  195.0 143.2 %all-to-all-start.1 = ((bf16[32,32,3072]{2,1,0:T(8,128)(2,1)}), bf16[32,32,3072]{2,1,0:T(8,128)(2,1)}, u32[]{:S(2)}, u32[]{:S(2)}) async-start(bf16[32,32,3072]{2,1,0:T(8,128)(2,1)} %bitcast.52), calls=%async_computation.1 | async-start | bytes 12582912 | tf_op jit(solution)/shard_map/all_to_all | solution.py:51
where the time goes:
time: 348 us; the launch traced here: 345 us
  waiting for transfers between devices  155 us (45%)
  blocking collectives  148 us (43%)
  matrix products  17.2 us (5%)
  starting transfers between devices  11.8 us (3%)
  other arithmetic  7.8 us (2%)
  local copies, waits for them, and re-layouts  4.88 us (1%)
    all_to_all x1, blocking collectives, local(): lax.all_to_all(outgoing, 'expert', split_axis=0, concat_axis=0, tiled=True)  148 us
    all_to_all x1, waiting for transfers between devices, local(): lax.all_to_all(partial_value.reshape(received.shape), 'expert', split_axi...  136 us
    ppermute x1, waiting for transfers between devices, passed_along(): return lax.ppermute(value, axis, pairs)  19.2 us
    dot_general x1, matrix products, local(): jnp.dot(hidden, w_down[0], preferred_element_type=jnp.float32)  11 us
  transfers between devices with their start and end apart: 2, of which 2 were waited for; matrix products, arithmetic and copies ran while one was open for 1% of the time, Pallas kernels for 0%

commit v1 on v0

v1 whole, which is shorter than its diff:
```python
import jax
import jax.numpy as jnp
from jax import lax
from jax.experimental import pallas as pl
from jax.experimental.pallas import tpu as pltpu
from jax.sharding import PartitionSpec as P

D = 3072
HS = 192
EXPERTS = 4
CAP = 32
TOK = 128
NX = 4
NY = 8
C = 512
J = D // C
HALF = C // 2
DHALF = HS // 2
MESH = pl.DeviceIdType.MESH
F32 = jnp.float32
BF16 = jnp.bfloat16


def kernel(
    blocks, gain, w_gate, w_up, w_down, ids, weights, out,
    arrived, picked, rows, wgu, wd, gate_in, up_in, acc, ssq, home_ssq,
    hidden, own_part, pair_out, pair_in, home_out, home_in, out_buf,
    gather_m, combine_hi, combine_lo, zero_w, home_inv,
    load_sem, store_sem, relay_s, relay_r, disp_s, disp_r, pair_s, pair_r,
    gx_s, gx_r, gf_s, gf_r, gd_s, gd_r, dx_s, dx_r, df_s, df_r, dd_s, dd_r,
    back_s, back_r, ret_s, ret_r,
):
    section = lax.axis_index("section")
    sections = lax.axis_size("section")
    place = lax.axis_index("expert")
    core = lax.axis_index("dp")
    y = place // NX
    x = place % NX
    sign = 2 * (y % 2) - 1

    def at_x(step):
        return {"expert": y * NX + (x + step + NX) % NX}

    def at_y(step):
        return {"expert": ((y + step + NY) % NY) * NX + x}

    next_section = {"section": (section + 1) % sections}
    last_section = {"section": (section + sections - 1) % sections}
    other_core = {"dp": 1 - core}
    pair = at_y(-sign)

    def remote(src, dst, send, recv, target):
        return pltpu.make_async_remote_copy(
            src_ref=src, dst_ref=dst, send_sem=send, recv_sem=recv,
            device_id=target, device_id_type=MESH,
        )

    def cols(j):
        return pl.ds(pl.multiple_of(j * C, C), C)

    def load_gate(j):
        return pltpu.make_async_copy(w_gate.at[0, cols(j), :], gate_in.at[j], load_sem.at[0, j])

    def load_up(j):
        return pltpu.make_async_copy(w_up.at[0, cols(j), :], up_in.at[j], load_sem.at[1, j])

    def load_down(j):
        return pltpu.make_async_copy(w_down.at[0, :, cols(j)], wd.at[0, j], load_sem.at[2, j])

    def store_out(j):
        return pltpu.make_async_copy(out_buf.at[j], out.at[0, :, cols(j)], store_sem.at[j])

    def relay(j):
        return remote(blocks.at[0, :, cols(j)], arrived.at[j], relay_s.at[j], relay_r.at[j], next_section)

    def dispatch(d, j):
        step = (sign, -2 * sign, 3 * sign)[d - 1]
        part = pl.ds(d * CAP, CAP)
        return remote(
            picked.at[j, part, :], rows.at[j, part, :], disp_s.at[d - 1, j], disp_r.at[d - 1, j], at_y(step)
        )

    def keep(j):
        return pltpu.make_async_copy(
            picked.at[j, pl.ds(0, CAP), :], rows.at[j, pl.ds(0, CAP), :], load_sem.at[3, j]
        )

    def to_pair(j):
        return remote(
            rows.at[j, pl.ds(0, TOK), :], rows.at[j, pl.ds(TOK, TOK), :], pair_s.at[j], pair_r.at[j], pair
        )

    def ring(buf, count, sx, rx, sf, rf, sd, rd):
        mine = pl.ds(pl.multiple_of(core * count, count), count)

        def own(k, j):
            return remote(
                buf.at[0, j, mine, :], buf.at[(3, 1)[k], j, mine, :], sx.at[k, j], rx.at[k, j], at_x((1, -1)[k])
            )

        def forward(j):
            return remote(
                buf.at[3 - 2 * core, j, mine, :], buf.at[2, j, mine, :], sf.at[j], rf.at[j], at_x(1 - 2 * core)
            )

        def share(s, j):
            here = buf.at[s, j, mine, :]
            return remote(here, here, sd.at[s - 1, j], rd.at[s - 1, j], other_core)

        def share_in(s, j):
            theirs = buf.at[s, j, pl.ds(pl.multiple_of((1 - core) * count, count), count), :]
            return remote(theirs, theirs, sd.at[s - 1, j], rd.at[s - 1, j], other_core)

        return own, forward, share, share_in

    g_own, g_forward, g_share, g_share_in = ring(wgu, HALF, gx_s, gx_r, gf_s, gf_r, gd_s, gd_r)
    d_own, d_forward, d_share, d_share_in = ring(wd, DHALF, dx_s, dx_r, df_s, df_r, dd_s, dd_r)

    def back_to_pair(j):
        return remote(pair_out.at[j], pair_in.at[j], back_s.at[j], back_r.at[j], pair)

    def go_home(d, j):
        part = pl.ds(d * CAP, CAP)
        return remote(
            home_out.at[j, part, :], home_in.at[j, part, :], ret_s.at[d - 1, j], ret_r.at[d - 1, j], at_y(d * sign)
        )

    def keep_home(j):
        return pltpu.make_async_copy(
            home_out.at[j, pl.ds(0, CAP), :], home_in.at[j, pl.ds(0, CAP), :], load_sem.at[4, j]
        )

    def each(fn):
        def body(j, carry):
            fn(j)
            return carry
        lax.fori_loop(0, J, body, 0)

    def staged(length, stages):
        def body(t, carry):
            for lag, fn in stages:
                @pl.when((t >= lag) & (t < lag + J))
                def _(fn=fn, lag=lag):
                    fn(t - lag)
            return carry
        lax.fori_loop(0, length, body, 0)

    def start_loads(j):
        load_gate(j).start()
        load_up(j).start()

    each(start_loads)
    each(lambda j: load_down(j).start())

    barrier = pltpu.get_barrier_semaphore()
    partners = [
        next_section, last_section, other_core, at_x(1), at_x(-1),
        at_y(1), at_y(-1), at_y(2), at_y(-2), at_y(3 * sign),
    ]
    for partner in partners:
        pl.semaphore_signal(barrier, inc=1, device_id=partner, device_id_type=MESH)
    pl.semaphore_wait(barrier, len(partners))

    each(lambda j: relay(j).start())

    def pack(j):
        load_gate(j).wait()
        load_up(j).wait()
        gate = gate_in[j]
        up = up_in[j]
        wgu[0, j, :, 0:128] = gate[:, 0:128]
        wgu[0, j, :, 128:256] = up[:, 0:128]
        wgu[0, j, :, 256:384] = jnp.concatenate([gate[:, 128:192], up[:, 128:192]], axis=1)
        g_own(0, j).start()
        g_own(1, j).start()

    each(pack)

    lane = lax.broadcasted_iota(jnp.int32, (TOK, TOK), 1)
    row = lax.broadcasted_iota(jnp.int32, (TOK, TOK), 0)
    group = lane // CAP
    hop = jnp.where(group == 0, 0, jnp.where(group == 1, sign, jnp.where(group == 2, -2 * sign, 3 * sign)))
    slot_expert = ((y + hop + NY) % NY) // 2
    first = ids[0, :, 0:1] == slot_expert
    second = ids[0, :, 1:2] == slot_expert
    member = jnp.where(first | second, 1.0, 0.0)
    earlier = jnp.where(lane < row, 1.0, 0.0).astype(BF16)
    rank = jnp.dot(earlier, member.astype(BF16), preferred_element_type=F32)
    slot = (lane % CAP).astype(F32)
    table = jnp.where(rank == slot, member, 0.0)
    gather_m[...] = table.T.astype(BF16)
    weighted = table * jnp.where(first, weights[0, :, 0:1], weights[0, :, 1:2])
    high = weighted.astype(BF16)
    combine_hi[...] = high
    combine_lo[...] = (weighted - high.astype(F32)).astype(BF16)
    zero_pick = jnp.where(ids[0] >= EXPERTS, weights[0], 0.0)
    zero_w[...] = jnp.broadcast_to(jnp.sum(zero_pick, axis=1, keepdims=True), (TOK, 128))

    acc[...] = jnp.zeros_like(acc)
    ssq[...] = jnp.zeros_like(ssq)
    home_ssq[...] = jnp.zeros_like(home_ssq)

    def squares(value):
        total = value[:, 0:128] * value[:, 0:128]
        for k in range(1, C // 128):
            piece = value[:, k * 128:(k + 1) * 128]
            total = total + piece * piece
        return total

    def pick_rows(j):
        relay(j).wait_recv()
        block = arrived[j]
        picked[j] = jnp.dot(gather_m[...], block, preferred_element_type=F32).astype(BF16)
        for d in (3, 2, 1):
            dispatch(d, j).start()
        keep(j).start()
        home_ssq[...] += squares(block.astype(F32))

    def pass_weights(j):
        g_own(0, j).wait_recv()
        g_own(1, j).wait_recv()
        g_forward(j).start()
        g_share(3, j).start()
        g_share(1, j).start()

    def pass_rows(j):
        keep(j).wait()
        for d in (1, 2, 3):
            dispatch(d, j).wait_recv()
        to_pair(j).start()

    def share_far(j):
        g_forward(j).wait_recv()
        g_share(2, j).start()

    def first_dots(j):
        to_pair(j).wait_recv()
        for s in (1, 3, 2):
            g_share_in(s, j).wait_recv()
        value = rows[j].astype(F32)
        ssq[...] += squares(value)
        scaled = (value * gain[0:1, cols(j)].astype(F32)).astype(BF16)
        for s in range(NX):
            acc[s] += jnp.dot(scaled, wgu[s, j], preferred_element_type=F32)

    def send_down(j):
        load_down(j).wait()
        d_own(0, j).start()
        d_own(1, j).start()

    staged(
        J + 3,
        [(0, pick_rows), (0, pass_weights), (0, pass_rows), (1, share_far), (3, send_down), (2, first_dots)],
    )

    inverse = lax.rsqrt(jnp.sum(ssq[...], axis=1, keepdims=True) * (1.0 / D) + 1e-06)
    for s in range(NX):
        act = acc[s] * inverse
        gate = act[:, 0:128]
        hidden[s, :, 0:128] = (gate / (1.0 + jnp.exp(-gate)) * act[:, 128:256]).astype(BF16)
        tail = act[:, 256:384]
        tail = tail / (1.0 + jnp.exp(-tail)) * pltpu.roll(tail, 64, 1)
        hidden[s, :, 128:192] = tail[:, 0:64].astype(BF16)
    home_inv[...] = jnp.broadcast_to(
        lax.rsqrt(jnp.sum(home_ssq[...], axis=1, keepdims=True) * (1.0 / D) + 1e-06), (TOK, 128)
    )

    def pass_down(j):
        d_own(0, j).wait_recv()
        d_own(1, j).wait_recv()
        d_forward(j).start()
        d_share(3, j).start()
        d_share(1, j).start()

    def share_down(j):
        d_forward(j).wait_recv()
        d_share(2, j).start()

    def half_dots(begin, j):
        total = jnp.dot(hidden[0, begin:begin + TOK, :], wd[0, j], preferred_element_type=F32)
        for s in range(1, NX):
            total = total + jnp.dot(hidden[s, begin:begin + TOK, :], wd[s, j], preferred_element_type=F32)
        return total

    def second_dots(j):
        for s in (1, 3, 2):
            d_share_in(s, j).wait_recv()
        pair_out[j] = half_dots(TOK, j).astype(BF16)
        back_to_pair(j).start()
        own_part[j] = half_dots(0, j)

    def add_pair(j):
        back_to_pair(j).wait_recv()
        home_out[j] = (own_part[j] + pair_in[j].astype(F32)).astype(BF16)
        for d in (3, 2, 1):
            go_home(d, j).start()
        keep_home(j).start()

    def finish(j):
        keep_home(j).wait()
        for d in (1, 2, 3):
            go_home(d, j).wait_recv()
        value = home_in[j]
        total = jnp.dot(combine_hi[...], value, preferred_element_type=F32)
        total = total + jnp.dot(combine_lo[...], value, preferred_element_type=F32)
        residual = arrived[j].astype(F32)
        normed = (residual * home_inv[:, 0:1] * gain[0:1, cols(j)].astype(F32)).astype(BF16)
        total = residual + zero_w[:, 0:1] * normed.astype(F32) + total
        out_buf[j] = total.astype(BF16)
        store_out(j).start()

    staged(J + 5, [(0, pass_down), (1, share_down), (2, second_dots), (3, add_pair), (5, finish)])

    def drain(j):
        store_out(j).wait()
        relay(j).wait_send()
        for d in (1, 2, 3):
            dispatch(d, j).wait_send()
            go_home(d, j).wait_send()
        to_pair(j).wait_send()
        back_to_pair(j).wait_send()
        for own, forward, share in ((g_own, g_forward, g_share), (d_own, d_forward, d_share)):
            own(0, j).wait_send()
            own(1, j).wait_send()
            forward(j).wait_send()
            for s in (1, 2, 3):
                share(s, j).wait_send()

    each(drain)


def local(blocks, norm_gain, w_gate, w_up, w_down, route_ids, route_weights):
    anywhere = pl.BlockSpec(memory_space=pl.ANY)
    vmem = pl.BlockSpec(memory_space=pltpu.VMEM)
    dma = pltpu.SemaphoreType.DMA
    return pl.pallas_call(
        kernel,
        out_shape=jax.ShapeDtypeStruct(blocks.shape, blocks.dtype),
        in_specs=[anywhere, vmem, anywhere, anywhere, anywhere, vmem, vmem],
        out_specs=anywhere,
        scratch_shapes=[
            pltpu.VMEM((J, TOK, C), BF16),
            pltpu.VMEM((J, TOK, C), BF16),
            pltpu.VMEM((J, 2 * TOK, C), BF16),
            pltpu.VMEM((NX, J, C, 2 * HS), BF16),
            pltpu.VMEM((NX, J, HS, C), BF16),
            pltpu.VMEM((J, C, HS), BF16),
            pltpu.VMEM((J, C, HS), BF16),
            pltpu.VMEM((NX, 2 * TOK, 2 * HS), F32),
            pltpu.VMEM((2 * TOK, 128), F32),
            pltpu.VMEM((TOK, 128), F32),
            pltpu.VMEM((NX, 2 * TOK, HS), BF16),
            pltpu.VMEM((J, TOK, C), F32),
            pltpu.VMEM((J, TOK, C), BF16),
            pltpu.VMEM((J, TOK, C), BF16),
            pltpu.VMEM((J, TOK, C), BF16),
            pltpu.VMEM((J, TOK, C), BF16),
            pltpu.VMEM((J, TOK, C), BF16),
            pltpu.VMEM((TOK, TOK), BF16),
            pltpu.VMEM((TOK, TOK), BF16),
            pltpu.VMEM((TOK, TOK), BF16),
            pltpu.VMEM((TOK, 128), F32),
            pltpu.VMEM((TOK, 128), F32),
            dma((5, J)), dma((J,)),
            dma((J,)), dma((J,)), dma((3, J)), dma((3, J)), dma((J,)), dma((J,)),
            dma((2, J)), dma((2, J)), dma((J,)), dma((J,)), dma((3, J)), dma((3, J)),
            dma((2, J)), dma((2, J)), dma((J,)), dma((J,)), dma((3, J)), dma((3, J)),
            dma((J,)), dma((J,)), dma((3, J)), dma((3, J)),
        ],
        compiler_params=pltpu.CompilerParams(
            collective_id=0, has_side_effects=True, vmem_limit_bytes=50 * 1024 * 1024
        ),
        cost_estimate=pl.CostEstimate(
            flops=2 * 3 * 1024 * D * HS, bytes_accessed=6 * 1024 * 1024, transcendentals=256 * 768
        ),
    )(blocks, norm_gain, w_gate, w_up, w_down, route_ids, route_weights)


def solution(mesh):
    placed = (
        P("section", ("dp", "expert"), None),
        P("section", None),
        P("section", None, "expert"),
        P("section", None, "expert"),
        P("section", "expert", None),
        P("section", ("dp", "expert"), None),
        P("section", ("dp", "expert"), None),
    )
    return jax.shard_map(
        local,
        mesh=mesh,
        in_specs=placed,
        out_specs=P("section", ("dp", "expert"), None),
        check_vma=False,
    )
```

time: 348 us -> 120 us (0.34)
  waiting for transfers between devices: 155 us -> 0 us
  blocking collectives: 148 us -> 0 us
  Pallas kernels: 0 us -> 113 us
  matrix products: 17.2 us -> 0 us
  starting transfers between devices: 11.8 us -> 0 us
  other arithmetic: 7.8 us -> 0 us
    all_to_all x1 -> x0, blocking collectives: 148 us -> none  [local(): lax.all_to_all(outgoing, 'expert', split_axis=0, concat_axis=0, tiled=True)]
    all_to_all x1 -> x0, waiting for transfers between devices: 136 us -> none  [local(): lax.all_to_all(partial_value.reshape(received.shape), 'expert', split_axi...]
    pallas_call x0 -> x1, Pallas kernels: none -> 113 us  [local(): pl.pallas_call(kernel, out_shape=jax.ShapeDtypeStruct(blocks.shape, block...]
    ppermute x1 -> x0, waiting for transfers between devices: 19.2 us -> none  [passed_along(): return lax.ppermute(value, axis, pairs)]
    dot_general x4 -> x0, matrix products: 17.2 us -> none  [the longest x1 11 us: local(): jnp.dot(hidden, w_down[0], preferred_element_type=jnp.float32)]
    all_to_all x1 -> x0, starting transfers between devices: 6.87 us -> none  [local(): lax.all_to_all(partial_value.reshape(received.shape), 'expert', split_axi...]
    reduce_sum x4 -> x0, other arithmetic: 5.02 us -> none  [the longest x1 4.04 us: local(): jnp.sum(returned.reshape(experts, slice_count, CAP, returned.shape[-1]).a...]
    ppermute x1 -> x0, starting transfers between devices: 4.95 us -> none  [passed_along(): return lax.ppermute(value, axis, pairs)]
  transfers between devices with their start and end apart: 2 -> 0, of which waited for: 2 -> 0; matrix products, arithmetic and copies ran while one was open for 1% -> 0% of each run, Pallas kernels for 0% -> 0%
where the time goes in v1:
time: 120 us
  Pallas kernels  113 us (94%)
  local copies, waits for them, and re-layouts  6.99 us (6%)
    pallas_call x1, Pallas kernels, local(): pl.pallas_call(kernel, out_shape=jax.ShapeDtypeStruct(blocks.shape, block...  113 us
    unnamed x13, local copies, waits for them, and re-layouts  6.99 us

profile of v1, /device:TPU:1, one launch (start us, length us, event | category | flops | bytes accessed | tf_op | source)
XLA Modules:
  0.0 119.6 jit_solution(8200734667248270480)
XLA Ops:
  0.0 0.8 copy.10.ids
  0.8 0.8 copy.11.weights
  1.6 0.0 copy-start.3
  1.6 2.6 %copy.8.w_gate = bf16[1,3072,192]{2,1,0:T(8,128)(2,1)} copy(bf16[1,3072,192]{1,2,0:T(8,128)(2,1)} %param.9) | data formatting | bytes 2359296 | tf_op args[2]
  4.2 0.0 copy-done.3
  4.2 0.0 copy-start
  4.2 0.0 copy-start.1
  4.2 0.0 copy-start.2
  4.2 1.6 %copy.9.w_up = bf16[1,3072,192]{2,1,0:T(8,128)(2,1)} copy(bf16[1,3072,192]{1,2,0:T(8,128)(2,1)S(1)} %copy-done.3) | data formatting | bytes 2359296 | tf_op args[3]
  5.8 0.0 copy-done
  5.8 0.4 copy-done.1
  6.1 0.0 copy-done.2
  6.1 112.6 %shard_map.73 = bf16[1,128,3072]{2,1,0:T(8,128)(2,1)S(1)} custom-call(bf16[1,128,3072]{2,1,0:T(8,128)(2,1)S(1)} %copy-done.1, bf16[1,3072]{1,0:T(2,128)(2,1)S(1)} %copy-done.2, bf16[1,3072,192]{2,1,0:T(8,128)(2,1)} %copy.8.w_gate, bf16[1,3072,192]{2,1,0:T(8,128)(2,1)} %copy.9.w_up, bf16[1,192,3072]{2,1,0:T(8,128)(2,1)S(1)} %copy-done, ...), custom_call_target="tpu_custom_call" | custom-call | flops 3623878656 | bytes 6291456 | tf_op jit(solution)/shard_map/pallas_call | solution.py:336
  118.7 0.9 copy.13
Async XLA Ops:
  1.6 2.6 %copy-start.3 = (bf16[1,3072,192]{1,2,0:T(8,128)(2,1)S(1)}, bf16[1,3072,192]{1,2,0:T(8,128)(2,1)}, u32[]{:S(2)}) copy-start(bf16[1,3072,192]{1,2,0:T(8,128)(2,1)} %param.10) | copy-start | bytes 3538948
  4.2 1.6 %copy-start = (bf16[1,192,3072]{2,1,0:T(8,128)(2,1)S(1)}, bf16[1,192,3072]{2,1,0:T(8,128)(2,1)}, u32[]{:S(2)}) copy-start(bf16[1,192,3072]{2,1,0:T(8,128)(2,1)} %w_down.1) | copy-start | bytes 3538948
  4.2 1.9 %copy-start.1 = (bf16[1,128,3072]{2,1,0:T(8,128)(2,1)S(1)}, bf16[1,128,3072]{2,1,0:T(8,128)(2,1)}, u32[]{:S(2)}) copy-start(bf16[1,128,3072]{2,1,0:T(8,128)(2,1)} %blocks.1) | copy-start | bytes 2359300
  4.2 1.9 %copy-start.2 = (bf16[1,3072]{1,0:T(2,128)(2,1)S(1)}, bf16[1,3072]{1,0:T(2,128)(2,1)}, u32[]{:S(2)}) copy-start(bf16[1,3072]{1,0:T(2,128)(2,1)} %gain.1) | copy-start | bytes 18436

commit v2 on v1

--- a/solution.py
+++ b/solution.py
@@ -14,7 +14,6 @@
 NY = 8
 C = 512
 J = D // C
-HALF = C // 2
 DHALF = HS // 2
 MESH = pl.DeviceIdType.MESH
 F32 = jnp.float32
@@ -23,7 +22,7 @@
 
 def kernel(
     blocks, gain, w_gate, w_up, w_down, ids, weights, out,
-    arrived, picked, rows, wgu, wd, gate_in, up_in, acc, ssq, home_ssq,
+    arrived, picked, rows, wgu, wd, acc, ssq, home_ssq,
     hidden, own_part, pair_out, pair_in, home_out, home_in, out_buf,
     gather_m, combine_hi, combine_lo, zero_w, home_inv,
     load_sem, store_sem, relay_s, relay_r, disp_s, disp_r, pair_s, pair_r,
@@ -59,13 +58,13 @@
         return pl.ds(pl.multiple_of(j * C, C), C)
 
     def load_gate(j):
-        return pltpu.make_async_copy(w_gate.at[0, cols(j), :], gate_in.at[j], load_sem.at[0, j])
+        return pltpu.make_async_copy(w_gate.at[0, :, cols(j)], wgu.at[j, 0, pl.ds(0, HS), :], load_sem.at[0, j])
 
     def load_up(j):
-        return pltpu.make_async_copy(w_up.at[0, cols(j), :], up_in.at[j], load_sem.at[1, j])
+        return pltpu.make_async_copy(w_up.at[0, :, cols(j)], wgu.at[j, 0, pl.ds(HS, HS), :], load_sem.at[1, j])
 
     def load_down(j):
-        return pltpu.make_async_copy(w_down.at[0, :, cols(j)], wd.at[0, j], load_sem.at[2, j])
+        return pltpu.make_async_copy(w_down.at[0, :, cols(j)], wd.at[j, 0], load_sem.at[2, j])
 
     def store_out(j):
         return pltpu.make_async_copy(out_buf.at[j], out.at[0, :, cols(j)], store_sem.at[j])
@@ -95,25 +94,25 @@
 
         def own(k, j):
             return remote(
-                buf.at[0, j, mine, :], buf.at[(3, 1)[k], j, mine, :], sx.at[k, j], rx.at[k, j], at_x((1, -1)[k])
+                buf.at[j, 0, mine, :], buf.at[j, (3, 1)[k], mine, :], sx.at[k, j], rx.at[k, j], at_x((1, -1)[k])
             )
 
         def forward(j):
             return remote(
-                buf.at[3 - 2 * core, j, mine, :], buf.at[2, j, mine, :], sf.at[j], rf.at[j], at_x(1 - 2 * core)
+                buf.at[j, 3 - 2 * core, mine, :], buf.at[j, 2, mine, :], sf.at[j], rf.at[j], at_x(1 - 2 * core)
             )
 
         def share(s, j):
-            here = buf.at[s, j, mine, :]
+            here = buf.at[j, s, mine, :]
             return remote(here, here, sd.at[s - 1, j], rd.at[s - 1, j], other_core)
 
         def share_in(s, j):
-            theirs = buf.at[s, j, pl.ds(pl.multiple_of((1 - core) * count, count), count), :]
+            theirs = buf.at[j, s, pl.ds(pl.multiple_of((1 - core) * count, count), count), :]
             return remote(theirs, theirs, sd.at[s - 1, j], rd.at[s - 1, j], other_core)
 
         return own, forward, share, share_in
 
-    g_own, g_forward, g_share, g_share_in = ring(wgu, HALF, gx_s, gx_r, gf_s, gf_r, gd_s, gd_r)
+    g_own, g_forward, g_share, g_share_in = ring(wgu, HS, gx_s, gx_r, gf_s, gf_r, gd_s, gd_r)
     d_own, d_forward, d_share, d_share_in = ring(wd, DHALF, dx_s, dx_r, df_s, df_r, dd_s, dd_r)
 
     def back_to_pair(j):
@@ -163,38 +162,34 @@
 
     each(lambda j: relay(j).start())
 
-    def pack(j):
+    def send_first(j):
         load_gate(j).wait()
         load_up(j).wait()
-        gate = gate_in[j]
-        up = up_in[j]
-        wgu[0, j, :, 0:128] = gate[:, 0:128]
-        wgu[0, j, :, 128:256] = up[:, 0:128]
-        wgu[0, j, :, 256:384] = jnp.concatenate([gate[:, 128:192], up[:, 128:192]], axis=1)
         g_own(0, j).start()
         g_own(1, j).start()
 
-    each(pack)
+    each(send_first)
 
     lane = lax.broadcasted_iota(jnp.int32, (TOK, TOK), 1)
     row = lax.broadcasted_iota(jnp.int32, (TOK, TOK), 0)
-    group = lane // CAP
+    group = row // CAP
     hop = jnp.where(group == 0, 0, jnp.where(group == 1, sign, jnp.where(group == 2, -2 * sign, 3 * sign)))
     slot_expert = ((y + hop + NY) % NY) // 2
-    first = ids[0, :, 0:1] == slot_expert
-    second = ids[0, :, 1:2] == slot_expert
+    first = ids[0, 0:1, :] == slot_expert
+    second = ids[0, 1:2, :] == slot_expert
     member = jnp.where(first | second, 1.0, 0.0)
-    earlier = jnp.where(lane < row, 1.0, 0.0).astype(BF16)
-    rank = jnp.dot(earlier, member.astype(BF16), preferred_element_type=F32)
-    slot = (lane % CAP).astype(F32)
+    earlier = jnp.where(row < lane, 1.0, 0.0).astype(BF16)
+    rank = jnp.dot(member.astype(BF16), earlier, preferred_element_type=F32)
+    slot = (row % CAP).astype(F32)
     table = jnp.where(rank == slot, member, 0.0)
-    gather_m[...] = table.T.astype(BF16)
-    weighted = table * jnp.where(first, weights[0, :, 0:1], weights[0, :, 1:2])
+    gather_m[...] = table.astype(BF16)
+    weighted = (table * jnp.where(first, weights[0, 0:1, :], weights[0, 1:2, :])).T
     high = weighted.astype(BF16)
     combine_hi[...] = high
     combine_lo[...] = (weighted - high.astype(F32)).astype(BF16)
     zero_pick = jnp.where(ids[0] >= EXPERTS, weights[0], 0.0)
-    zero_w[...] = jnp.broadcast_to(jnp.sum(zero_pick, axis=1, keepdims=True), (TOK, 128))
+    zero_sum = jnp.sum(zero_pick, axis=0, keepdims=True)
+    zero_w[...] = jnp.broadcast_to(zero_sum, (TOK, TOK)).T
 
     acc[...] = jnp.zeros_like(acc)
     ssq[...] = jnp.zeros_like(ssq)
@@ -240,8 +235,9 @@
         value = rows[j].astype(F32)
         ssq[...] += squares(value)
         scaled = (value * gain[0:1, cols(j)].astype(F32)).astype(BF16)
-        for s in range(NX):
-            acc[s] += jnp.dot(scaled, wgu[s, j], preferred_element_type=F32)
+        acc[...] += lax.dot_general(
+            scaled, wgu[j].reshape(NX * 2 * HS, C), (((1,), (1,)), ((), ())), preferred_element_type=F32
+        )
 
     def send_down(j):
         load_down(j).wait()
@@ -254,13 +250,14 @@
     )
 
     inverse = lax.rsqrt(jnp.sum(ssq[...], axis=1, keepdims=True) * (1.0 / D) + 1e-06)
+    low = lax.broadcasted_iota(jnp.int32, (2 * TOK, 128), 1) < 64
     for s in range(NX):
-        act = acc[s] * inverse
-        gate = act[:, 0:128]
-        hidden[s, :, 0:128] = (gate / (1.0 + jnp.exp(-gate)) * act[:, 128:256]).astype(BF16)
-        tail = act[:, 256:384]
-        tail = tail / (1.0 + jnp.exp(-tail)) * pltpu.roll(tail, 64, 1)
-        hidden[s, :, 128:192] = tail[:, 0:64].astype(BF16)
+        base = s * 2 * HS
+        gate = acc[:, base:base + 128] * inverse
+        mid = acc[:, base + 128:base + 256] * inverse
+        up = pltpu.roll(acc[:, base + 256:base + 384] * inverse, 64, 1)
+        hidden[s, :, 0:128] = (gate / (1.0 + jnp.exp(-gate)) * jnp.where(low, pltpu.roll(mid, 64, 1), up)).astype(BF16)
+        hidden[s, :, 128:192] = (mid / (1.0 + jnp.exp(-mid)) * up)[:, 0:64].astype(BF16)
     home_inv[...] = jnp.broadcast_to(
         lax.rsqrt(jnp.sum(home_ssq[...], axis=1, keepdims=True) * (1.0 / D) + 1e-06), (TOK, 128)
     )
@@ -277,9 +274,9 @@
         d_share(2, j).start()
 
     def half_dots(begin, j):
-        total = jnp.dot(hidden[0, begin:begin + TOK, :], wd[0, j], preferred_element_type=F32)
+        total = jnp.dot(hidden[0, begin:begin + TOK, :], wd[j, 0], preferred_element_type=F32)
         for s in range(1, NX):
-            total = total + jnp.dot(hidden[s, begin:begin + TOK, :], wd[s, j], preferred_element_type=F32)
+            total = total + jnp.dot(hidden[s, begin:begin + TOK, :], wd[j, s], preferred_element_type=F32)
         return total
 
     def second_dots(j):
@@ -342,11 +339,9 @@
             pltpu.VMEM((J, TOK, C), BF16),
             pltpu.VMEM((J, TOK, C), BF16),
             pltpu.VMEM((J, 2 * TOK, C), BF16),
-            pltpu.VMEM((NX, J, C, 2 * HS), BF16),
-            pltpu.VMEM((NX, J, HS, C), BF16),
-            pltpu.VMEM((J, C, HS), BF16),
-            pltpu.VMEM((J, C, HS), BF16),
-            pltpu.VMEM((NX, 2 * TOK, 2 * HS), F32),
+            pltpu.VMEM((J, NX, 2 * HS, C), BF16),
+            pltpu.VMEM((J, NX, HS, C), BF16),
+            pltpu.VMEM((2 * TOK, NX * 2 * HS), F32),
             pltpu.VMEM((2 * TOK, 128), F32),
             pltpu.VMEM((TOK, 128), F32),
             pltpu.VMEM((NX, 2 * TOK, HS), BF16),
@@ -373,7 +368,10 @@
         cost_estimate=pl.CostEstimate(
             flops=2 * 3 * 1024 * D * HS, bytes_accessed=6 * 1024 * 1024, transcendentals=256 * 768
         ),
-    )(blocks, norm_gain, w_gate, w_up, w_down, route_ids, route_weights)
+    )(
+        blocks, norm_gain, jnp.swapaxes(w_gate, 1, 2), jnp.swapaxes(w_up, 1, 2), w_down,
+        jnp.swapaxes(route_ids, 1, 2), jnp.swapaxes(route_weights, 1, 2),
+    )
 
 
 def solution(mesh):

time: 120 us -> 120 us (level)
  no operation moved by 1% of the time
where the time goes in v2:
time: 120 us; the launch traced here: 119 us
  Pallas kernels  112 us (93%)
  local copies, waits for them, and re-layouts  6.62 us (6%)
    pallas_call x1, Pallas kernels, local(): pl.pallas_call(kernel, out_shape=jax.ShapeDtypeStruct(blocks.shape, block...  112 us
    unnamed x13, local copies, waits for them, and re-layouts  6.62 us

profile of v2, /device:TPU:1, one launch (start us, length us, event | category | flops | bytes accessed | tf_op | source)
XLA Modules:
  0.0 118.9 jit_solution(13298247165922916420)
XLA Ops:
  0.0 0.0 copy-start
  0.0 1.3 %copy-done = bf16[1,3072,192]{1,2,0:T(8,128)(2,1)S(1)} copy-done((bf16[1,3072,192]{1,2,0:T(8,128)(2,1)S(1)}, bf16[1,3072,192]{1,2,0:T(8,128)(2,1)}, u32[]{:S(2)}) %copy-start) | copy-done | bytes 1179672
  1.3 0.0 copy-start.1
  1.3 1.3 %copy-done.1 = bf16[1,3072,192]{1,2,0:T(8,128)(2,1)S(1)} copy-done((bf16[1,3072,192]{1,2,0:T(8,128)(2,1)S(1)}, bf16[1,3072,192]{1,2,0:T(8,128)(2,1)}, u32[]{:S(2)}) %copy-start.1) | copy-done | bytes 1179672
  2.5 0.0 copy-start.2
  2.5 1.1 copy-done.2
  3.7 0.0 copy-start.3
  3.7 0.7 copy-done.3
  4.4 0.0 copy-start.4
  4.4 0.7 copy-done.4
  5.1 0.0 copy-start.5
  5.1 0.7 copy-done.5
  5.7 112.3 %shard_map.73 = bf16[1,128,3072]{2,1,0:T(8,128)(2,1)S(1)} custom-call(bf16[1,128,3072]{2,1,0:T(8,128)(2,1)S(1)} %copy-done.2, bf16[1,3072]{1,0:T(2,128)(2,1)S(1)} %copy-done.3, bf16[1,192,3072]{2,1,0:T(8,128)(2,1)S(1)} %bitcast.4, bf16[1,192,3072]{2,1,0:T(8,128)(2,1)S(1)} %bitcast.5, bf16[1,192,3072]{2,1,0:T(8,128)(2,1)} %w_down.1, ...), custom_call_target="tpu_custom_call" | custom-call | flops 3623878656 | bytes 6291456 | tf_op jit(solution)/shard_map/pallas_call | solution.py:333
  118.0 0.9 copy.9
Async XLA Ops:
  0.0 1.3 %copy-start = (bf16[1,3072,192]{1,2,0:T(8,128)(2,1)S(1)}, bf16[1,3072,192]{1,2,0:T(8,128)(2,1)}, u32[]{:S(2)}) copy-start(bf16[1,3072,192]{1,2,0:T(8,128)(2,1)} %param.9) | copy-start | bytes 3538948
  1.3 1.3 %copy-start.1 = (bf16[1,3072,192]{1,2,0:T(8,128)(2,1)S(1)}, bf16[1,3072,192]{1,2,0:T(8,128)(2,1)}, u32[]{:S(2)}) copy-start(bf16[1,3072,192]{1,2,0:T(8,128)(2,1)} %param.10) | copy-start | bytes 3538948
  2.5 1.1 copy-start.2
  3.7 0.7 copy-start.3
  4.4 0.7 copy-start.4
  5.1 0.7 copy-start.5

commit v3 on v2

--- a/solution.py
+++ b/solution.py
@@ -15,17 +15,18 @@
 C = 512
 J = D // C
 DHALF = HS // 2
+NEAR = 3 * 2 * HS
 MESH = pl.DeviceIdType.MESH
 F32 = jnp.float32
 BF16 = jnp.bfloat16
 
 
 def kernel(
-    blocks, gain, w_gate, w_up, w_down, ids, weights, out,
-    arrived, picked, rows, wgu, wd, acc, ssq, home_ssq,
+    blocks, gain_in, w_gate, w_up, w_down, ids_in, weights_in, out,
+    gain, ids, weights, arrived, picked, rows, wgu, wd, scaled, acc, ssq, home_ssq,
     hidden, own_part, pair_out, pair_in, home_out, home_in, out_buf,
     gather_m, combine_hi, combine_lo, zero_w, home_inv,
-    load_sem, store_sem, relay_s, relay_r, disp_s, disp_r, pair_s, pair_r,
+    small_sem, load_sem, store_sem, relay_s, relay_r, disp_s, disp_r, pair_s, pair_r,
     gx_s, gx_r, gf_s, gf_r, gd_s, gd_r, dx_s, dx_r, df_s, df_r, dd_s, dd_r,
     back_s, back_r, ret_s, ret_r,
 ):
@@ -94,12 +95,12 @@
 
         def own(k, j):
             return remote(
-                buf.at[j, 0, mine, :], buf.at[j, (3, 1)[k], mine, :], sx.at[k, j], rx.at[k, j], at_x((1, -1)[k])
+                buf.at[j, 0, mine, :], buf.at[j, 2 - k, mine, :], sx.at[k, j], rx.at[k, j], at_x((1, -1)[k])
             )
 
         def forward(j):
             return remote(
-                buf.at[j, 3 - 2 * core, mine, :], buf.at[j, 2, mine, :], sf.at[j], rf.at[j], at_x(1 - 2 * core)
+                buf.at[j, 2 - core, mine, :], buf.at[j, 3, mine, :], sf.at[j], rf.at[j], at_x(1 - 2 * core)
             )
 
         def share(s, j):
@@ -135,19 +136,25 @@
             return carry
         lax.fori_loop(0, J, body, 0)
 
-    def staged(length, stages):
+    def staged(steps, stages):
         def body(t, carry):
-            for lag, fn in stages:
-                @pl.when((t >= lag) & (t < lag + J))
+            for lag, first, fn in stages:
+                @pl.when((t >= lag + first) & (t < lag + J))
                 def _(fn=fn, lag=lag):
                     fn(t - lag)
             return carry
-        lax.fori_loop(0, length, body, 0)
+        lax.fori_loop(0, steps, body, 0)
 
     def start_loads(j):
         load_gate(j).start()
         load_up(j).start()
 
+    small = [
+        pltpu.make_async_copy(src, dst, small_sem.at[k])
+        for k, (src, dst) in enumerate(((ids_in.at[0], ids), (weights_in.at[0], weights), (gain_in, gain)))
+    ]
+    for copy in small:
+        copy.start()
     each(start_loads)
     each(lambda j: load_down(j).start())
 
@@ -158,42 +165,44 @@
     ]
     for partner in partners:
         pl.semaphore_signal(barrier, inc=1, device_id=partner, device_id_type=MESH)
-    pl.semaphore_wait(barrier, len(partners))
-
-    each(lambda j: relay(j).start())
-
-    def send_first(j):
-        load_gate(j).wait()
-        load_up(j).wait()
-        g_own(0, j).start()
-        g_own(1, j).start()
-
-    each(send_first)
-
+    for copy in small:
+        copy.wait()
     lane = lax.broadcasted_iota(jnp.int32, (TOK, TOK), 1)
     row = lax.broadcasted_iota(jnp.int32, (TOK, TOK), 0)
     group = row // CAP
     hop = jnp.where(group == 0, 0, jnp.where(group == 1, sign, jnp.where(group == 2, -2 * sign, 3 * sign)))
     slot_expert = ((y + hop + NY) % NY) // 2
-    first = ids[0, 0:1, :] == slot_expert
-    second = ids[0, 1:2, :] == slot_expert
+    first = ids[0:1, :] == slot_expert
+    second = ids[1:2, :] == slot_expert
     member = jnp.where(first | second, 1.0, 0.0)
     earlier = jnp.where(row < lane, 1.0, 0.0).astype(BF16)
     rank = jnp.dot(member.astype(BF16), earlier, preferred_element_type=F32)
     slot = (row % CAP).astype(F32)
     table = jnp.where(rank == slot, member, 0.0)
     gather_m[...] = table.astype(BF16)
-    weighted = (table * jnp.where(first, weights[0, 0:1, :], weights[0, 1:2, :])).T
+    weighted = (table * jnp.where(first, weights[0:1, :], weights[1:2, :])).T
     high = weighted.astype(BF16)
     combine_hi[...] = high
     combine_lo[...] = (weighted - high.astype(F32)).astype(BF16)
-    zero_pick = jnp.where(ids[0] >= EXPERTS, weights[0], 0.0)
+    zero_pick = jnp.where(ids[...] >= EXPERTS, weights[...], 0.0)
     zero_sum = jnp.sum(zero_pick, axis=0, keepdims=True)
     zero_w[...] = jnp.broadcast_to(zero_sum, (TOK, TOK)).T
 
     acc[...] = jnp.zeros_like(acc)
     ssq[...] = jnp.zeros_like(ssq)
     home_ssq[...] = jnp.zeros_like(home_ssq)
+
+    pl.semaphore_wait(barrier, len(partners))
+
+    each(lambda j: relay(j).start())
+
+    def send_first(j):
+        load_gate(j).wait()
+        load_up(j).wait()
+        g_own(0, j).start()
+        g_own(1, j).start()
+
+    each(send_first)
 
     def squares(value):
         total = value[:, 0:128] * value[:, 0:128]
@@ -215,8 +224,8 @@
         g_own(0, j).wait_recv()
         g_own(1, j).wait_recv()
         g_forward(j).start()
-        g_share(3, j).start()
         g_share(1, j).start()
+        g_share(2, j).start()
 
     def pass_rows(j):
         keep(j).wait()
@@ -226,17 +235,23 @@
 
     def share_far(j):
         g_forward(j).wait_recv()
-        g_share(2, j).start()
-
-    def first_dots(j):
+        g_share(3, j).start()
+
+    def near_dots(j):
         to_pair(j).wait_recv()
-        for s in (1, 3, 2):
-            g_share_in(s, j).wait_recv()
         value = rows[j].astype(F32)
         ssq[...] += squares(value)
-        scaled = (value * gain[0:1, cols(j)].astype(F32)).astype(BF16)
-        acc[...] += lax.dot_general(
-            scaled, wgu[j].reshape(NX * 2 * HS, C), (((1,), (1,)), ((), ())), preferred_element_type=F32
+        scaled[j] = (value * gain[0:1, cols(j)].astype(F32)).astype(BF16)
+        for s in (1, 2):
+            g_share_in(s, j).wait_recv()
+        acc[:, 0:NEAR] += lax.dot_general(
+            scaled[j], wgu[j, 0:3].reshape(NEAR, C), (((1,), (1,)), ((), ())), preferred_element_type=F32
+        )
+
+    def far_dots(j):
+        g_share_in(3, j).wait_recv()
+        acc[:, NEAR:] += lax.dot_general(
+            scaled[j], wgu[j, 3], (((1,), (1,)), ((), ())), preferred_element_type=F32
         )
 
     def send_down(j):
@@ -244,34 +259,47 @@
         d_own(0, j).start()
         d_own(1, j).start()
 
-    staged(
-        J + 3,
-        [(0, pick_rows), (0, pass_weights), (0, pass_rows), (1, share_far), (3, send_down), (2, first_dots)],
-    )
-
-    inverse = lax.rsqrt(jnp.sum(ssq[...], axis=1, keepdims=True) * (1.0 / D) + 1e-06)
-    low = lax.broadcasted_iota(jnp.int32, (2 * TOK, 128), 1) < 64
-    for s in range(NX):
-        base = s * 2 * HS
-        gate = acc[:, base:base + 128] * inverse
-        mid = acc[:, base + 128:base + 256] * inverse
-        up = pltpu.roll(acc[:, base + 256:base + 384] * inverse, 64, 1)
-        hidden[s, :, 0:128] = (gate / (1.0 + jnp.exp(-gate)) * jnp.where(low, pltpu.roll(mid, 64, 1), up)).astype(BF16)
-        hidden[s, :, 128:192] = (mid / (1.0 + jnp.exp(-mid)) * up)[:, 0:64].astype(BF16)
-    home_inv[...] = jnp.broadcast_to(
-        lax.rsqrt(jnp.sum(home_ssq[...], axis=1, keepdims=True) * (1.0 / D) + 1e-06), (TOK, 128)
-    )
-
     def pass_down(j):
         d_own(0, j).wait_recv()
         d_own(1, j).wait_recv()
         d_forward(j).start()
-        d_share(3, j).start()
         d_share(1, j).start()
+        d_share(2, j).start()
 
     def share_down(j):
         d_forward(j).wait_recv()
-        d_share(2, j).start()
+        d_share(3, j).start()
+
+    def activate(slots):
+        inverse = lax.rsqrt(jnp.sum(ssq[...], axis=1, keepdims=True) * (1.0 / D) + 1e-06)
+        low = lax.broadcasted_iota(jnp.int32, (2 * TOK, 128), 1) < 64
+        for s in slots:
+            base = s * 2 * HS
+            gate = acc[:, base:base + 128] * inverse
+            mid = acc[:, base + 128:base + 256] * inverse
+            up = pltpu.roll(acc[:, base + 256:base + 384] * inverse, 64, 1)
+            other = jnp.where(low, pltpu.roll(mid, 64, 1), up)
+            hidden[s, :, 0:128] = (gate / (1.0 + jnp.exp(-gate)) * other).astype(BF16)
+            hidden[s, :, 128:192] = (mid / (1.0 + jnp.exp(-mid)) * up)[:, 0:64].astype(BF16)
+
+    def activate_near(j):
+        activate(range(3))
+        home_inv[...] = jnp.broadcast_to(
+            lax.rsqrt(jnp.sum(home_ssq[...], axis=1, keepdims=True) * (1.0 / D) + 1e-06), (TOK, 128)
+        )
+
+    staged(J, [(0, 0, pick_rows), (1, 0, pass_rows), (0, 0, pass_weights), (2, 0, near_dots)])
+    pass_rows(J - 1)
+    send_down(0)
+    send_down(1)
+    staged(
+        J,
+        [(0, 0, share_far), (3 - J, J - 2, near_dots), (1, 0, far_dots), (4 - J, J - 1, activate_near)],
+    )
+    pass_down(0)
+    send_down(2)
+    far_dots(J - 1)
+    activate((3,))
 
     def half_dots(begin, j):
         total = jnp.dot(hidden[0, begin:begin + TOK, :], wd[j, 0], preferred_element_type=F32)
@@ -280,7 +308,7 @@
         return total
 
     def second_dots(j):
-        for s in (1, 3, 2):
+        for s in (1, 2, 3):
             d_share_in(s, j).wait_recv()
         pair_out[j] = half_dots(TOK, j).astype(BF16)
         back_to_pair(j).start()
@@ -306,7 +334,16 @@
         out_buf[j] = total.astype(BF16)
         store_out(j).start()
 
-    staged(J + 5, [(0, pass_down), (1, share_down), (2, second_dots), (3, add_pair), (5, finish)])
+    pass_down(1)
+    send_down(3)
+    share_down(0)
+    staged(
+        J + 3,
+        [
+            (0, 0, second_dots), (-2, 2, pass_down), (-4, 4, send_down), (-1, 1, share_down),
+            (1, 0, add_pair), (3, 0, finish),
+        ],
+    )
 
     def drain(j):
         store_out(j).wait()
@@ -328,19 +365,22 @@
 
 def local(blocks, norm_gain, w_gate, w_up, w_down, route_ids, route_weights):
     anywhere = pl.BlockSpec(memory_space=pl.ANY)
-    vmem = pl.BlockSpec(memory_space=pltpu.VMEM)
     dma = pltpu.SemaphoreType.DMA
     return pl.pallas_call(
         kernel,
         out_shape=jax.ShapeDtypeStruct(blocks.shape, blocks.dtype),
-        in_specs=[anywhere, vmem, anywhere, anywhere, anywhere, vmem, vmem],
+        in_specs=[anywhere] * 7,
         out_specs=anywhere,
         scratch_shapes=[
+            pltpu.VMEM((1, D), BF16),
+            pltpu.VMEM((2, TOK), jnp.int32),
+            pltpu.VMEM((2, TOK), F32),
             pltpu.VMEM((J, TOK, C), BF16),
             pltpu.VMEM((J, TOK, C), BF16),
             pltpu.VMEM((J, 2 * TOK, C), BF16),
             pltpu.VMEM((J, NX, 2 * HS, C), BF16),
             pltpu.VMEM((J, NX, HS, C), BF16),
+            pltpu.VMEM((J, 2 * TOK, C), BF16),
             pltpu.VMEM((2 * TOK, NX * 2 * HS), F32),
             pltpu.VMEM((2 * TOK, 128), F32),
             pltpu.VMEM((TOK, 128), F32),
@@ -356,14 +396,14 @@
             pltpu.VMEM((TOK, TOK), BF16),
             pltpu.VMEM((TOK, 128), F32),
             pltpu.VMEM((TOK, 128), F32),
-            dma((5, J)), dma((J,)),
+            dma((3,)), dma((5, J)), dma((J,)),
             dma((J,)), dma((J,)), dma((3, J)), dma((3, J)), dma((J,)), dma((J,)),
             dma((2, J)), dma((2, J)), dma((J,)), dma((J,)), dma((3, J)), dma((3, J)),
             dma((2, J)), dma((2, J)), dma((J,)), dma((J,)), dma((3, J)), dma((3, J)),
             dma((J,)), dma((J,)), dma((3, J)), dma((3, J)),
         ],
         compiler_params=pltpu.CompilerParams(
-            collective_id=0, has_side_effects=True, vmem_limit_bytes=50 * 1024 * 1024
+            collective_id=0, has_side_effects=True, vmem_limit_bytes=60 * 1024 * 1024
         ),
         cost_estimate=pl.CostEstimate(
             flops=2 * 3 * 1024 * D * HS, bytes_accessed=6 * 1024 * 1024, transcendentals=256 * 768

time: 120 us -> 98.5 us (0.82)
  Pallas kernels: 112 us -> 96.3 us
  local copies, waits for them, and re-layouts: 6.62 us -> 2.06 us
    pallas_call x1, Pallas kernels: 112 us -> 96.3 us  [local(): pl.pallas_call(kernel, out_shape=jax.ShapeDtypeStruct(blocks.shape, block...]
    unnamed x13 -> x1, local copies, waits for them, and re-layouts: 6.62 us -> 2.06 us
where the time goes in v3:
time: 98.5 us; the launch traced here: 98.3 us
  Pallas kernels  96.3 us (98%)
  local copies, waits for them, and re-layouts  2.06 us (2%)
    pallas_call x1, Pallas kernels, local(): pl.pallas_call(kernel, out_shape=jax.ShapeDtypeStruct(blocks.shape, block...  96.3 us
    unnamed x1, local copies, waits for them, and re-layouts  2.06 us

profile of v3, /device:TPU:1, one launch (start us, length us, event | category | flops | bytes accessed | tf_op | source)
XLA Modules:
  0.0 98.3 jit_solution(3901683135400601598)
XLA Ops:
  0.0 96.3 %shard_map.73 = bf16[1,128,3072]{2,1,0:T(8,128)(2,1)} custom-call(bf16[1,128,3072]{2,1,0:T(8,128)(2,1)} %blocks.1, bf16[1,3072]{1,0:T(2,128)(2,1)} %gain_in.1, bf16[1,192,3072]{2,1,0:T(8,128)(2,1)} %bitcast.4, bf16[1,192,3072]{2,1,0:T(8,128)(2,1)} %bitcast.5, bf16[1,192,3072]{2,1,0:T(8,128)(2,1)} %w_down.1, s32[1,2,128]{2,1,0:T(2,128)} %bitcast.6, ...), custom_call_target="tpu_custom_call" | custom-call | flops 3623878656 | bytes 6291456 | tf_op jit(solution)/shard_map/pallas_call | solution.py:369
  96.3 2.1 %copy.9 = bf16[1,128,3072]{2,1,0:T(8,128)(2,1)} copy(bf16[1,128,3072]{2,1,0:T(8,128)(2,1)} %shard_map.73) | data formatting | bytes 1572864

commit v4 on v3

--- a/solution.py
+++ b/solution.py
@@ -14,7 +14,9 @@
 NY = 8
 C = 512
 J = D // C
-DHALF = HS // 2
+C2 = 256
+WIDE = D // 2
+J2 = WIDE // C2
 NEAR = 3 * 2 * HS
 MESH = pl.DeviceIdType.MESH
 F32 = jnp.float32
@@ -24,11 +26,11 @@
 def kernel(
     blocks, gain_in, w_gate, w_up, w_down, ids_in, weights_in, out,
     gain, ids, weights, arrived, picked, rows, wgu, wd, scaled, acc, ssq, home_ssq,
-    hidden, own_part, pair_out, pair_in, home_out, home_in, out_buf,
+    hidden, pair_hidden, packed_out, packed_in, tail_two, home_out, home_in, out_buf,
     gather_m, combine_hi, combine_lo, zero_w, home_inv,
-    small_sem, load_sem, store_sem, relay_s, relay_r, disp_s, disp_r, pair_s, pair_r,
+    small_sem, load_sem, down_sem, store_sem, relay_s, relay_r, disp_s, disp_r, pair_s, pair_r,
     gx_s, gx_r, gf_s, gf_r, gd_s, gd_r, dx_s, dx_r, df_s, df_r, dd_s, dd_r,
-    back_s, back_r, ret_s, ret_r,
+    pd_s, pd_r, pc_s, pc_r, act_s, act_r, ret_s, ret_r,
 ):
     section = lax.axis_index("section")
     sections = lax.axis_size("section")
@@ -48,6 +50,7 @@
     last_section = {"section": (section + sections - 1) % sections}
     other_core = {"dp": 1 - core}
     pair = at_y(-sign)
+    half = y % 2
 
     def remote(src, dst, send, recv, target):
         return pltpu.make_async_remote_copy(
@@ -58,6 +61,9 @@
     def cols(j):
         return pl.ds(pl.multiple_of(j * C, C), C)
 
+    def cols2(side, j):
+        return pl.ds(pl.multiple_of(side * WIDE + j * C2, C2), C2)
+
     def load_gate(j):
         return pltpu.make_async_copy(w_gate.at[0, :, cols(j)], wgu.at[j, 0, pl.ds(0, HS), :], load_sem.at[0, j])
 
@@ -65,10 +71,12 @@
         return pltpu.make_async_copy(w_up.at[0, :, cols(j)], wgu.at[j, 0, pl.ds(HS, HS), :], load_sem.at[1, j])
 
     def load_down(j):
-        return pltpu.make_async_copy(w_down.at[0, :, cols(j)], wd.at[j, 0], load_sem.at[2, j])
+        return pltpu.make_async_copy(
+            w_down.at[0, :, cols2(half, j)], wd.at[j, 0, pl.ds(0, HS), :], down_sem.at[j]
+        )
 
     def store_out(j):
-        return pltpu.make_async_copy(out_buf.at[j], out.at[0, :, cols(j)], store_sem.at[j])
+        return pltpu.make_async_copy(out_buf.at[j], out.at[0, :, cols2(0, j)], store_sem.at[j])
 
     def relay(j):
         return remote(blocks.at[0, :, cols(j)], arrived.at[j], relay_s.at[j], relay_r.at[j], next_section)
@@ -82,7 +90,7 @@
 
     def keep(j):
         return pltpu.make_async_copy(
-            picked.at[j, pl.ds(0, CAP), :], rows.at[j, pl.ds(0, CAP), :], load_sem.at[3, j]
+            picked.at[j, pl.ds(0, CAP), :], rows.at[j, pl.ds(0, CAP), :], load_sem.at[2, j]
         )
 
     def to_pair(j):
@@ -114,32 +122,51 @@
         return own, forward, share, share_in
 
     g_own, g_forward, g_share, g_share_in = ring(wgu, HS, gx_s, gx_r, gf_s, gf_r, gd_s, gd_r)
-    d_own, d_forward, d_share, d_share_in = ring(wd, DHALF, dx_s, dx_r, df_s, df_r, dd_s, dd_r)
-
-    def back_to_pair(j):
-        return remote(pair_out.at[j], pair_in.at[j], back_s.at[j], back_r.at[j], pair)
-
-    def go_home(d, j):
-        part = pl.ds(d * CAP, CAP)
+    d_own, d_forward, d_share, d_share_in = ring(wd, HS, dx_s, dx_r, df_s, df_r, dd_s, dd_r)
+
+    def pair_down(j):
         return remote(
-            home_out.at[j, part, :], home_in.at[j, part, :], ret_s.at[d - 1, j], ret_r.at[d - 1, j], at_y(d * sign)
-        )
+            w_down.at[0, :, cols2(1 - half, j)], wd.at[j, 0, pl.ds(HS, HS), :], pd_s.at[j], pd_r.at[j], pair
+        )
+
+    def core_down(j):
+        part = wd.at[j, 0, pl.ds(HS, HS), :]
+        return remote(part, part, pc_s.at[j], pc_r.at[j], other_core)
+
+    def exchange(k):
+        part = pl.ds((0, 4)[k], (4, 2)[k])
+        return remote(packed_out.at[part], packed_in.at[part], act_s.at[k], act_r.at[k], pair)
+
+    def home(src_row, d, slot, step, j):
+        return remote(
+            home_out.at[j, pl.ds(src_row, CAP), :], home_in.at[half * J2 + j, pl.ds(d * CAP, CAP), :],
+            ret_s.at[slot, j], ret_r.at[d, half * J2 + j], at_y(step),
+        )
+
+    def homes(j):
+        near = [home(d * CAP, d, d - 1, d * sign, j) for d in (1, 2, 3)]
+        far = [home(TOK + d * CAP, d, 3 + d, -(1 + d) * sign, j) for d in range(4)]
+        return near + far
+
+    def home_arrival(d, g):
+        part = home_in.at[g, pl.ds(d * CAP, CAP), :]
+        return remote(part, part, ret_s.at[0, 0], ret_r.at[d, g], pair)
 
     def keep_home(j):
         return pltpu.make_async_copy(
-            home_out.at[j, pl.ds(0, CAP), :], home_in.at[j, pl.ds(0, CAP), :], load_sem.at[4, j]
-        )
-
-    def each(fn):
+            home_out.at[j, pl.ds(0, CAP), :], home_in.at[half * J2 + j, pl.ds(0, CAP), :], down_sem.at[J2 + j]
+        )
+
+    def each(fn, count=J):
         def body(j, carry):
             fn(j)
             return carry
-        lax.fori_loop(0, J, body, 0)
-
-    def staged(steps, stages):
+        lax.fori_loop(0, count, body, 0)
+
+    def staged(steps, stages, count=J):
         def body(t, carry):
             for lag, first, fn in stages:
-                @pl.when((t >= lag + first) & (t < lag + J))
+                @pl.when((t >= lag + first) & (t < lag + count))
                 def _(fn=fn, lag=lag):
                     fn(t - lag)
             return carry
@@ -156,13 +183,10 @@
     for copy in small:
         copy.start()
     each(start_loads)
-    each(lambda j: load_down(j).start())
+    each(lambda j: load_down(j).start(), J2)
 
     barrier = pltpu.get_barrier_semaphore()
-    partners = [
-        next_section, last_section, other_core, at_x(1), at_x(-1),
-        at_y(1), at_y(-1), at_y(2), at_y(-2), at_y(3 * sign),
-    ]
+    partners = [next_section, last_section, other_core, at_x(1), at_x(-1)] + [at_y(k) for k in range(1, NY)]
     for partner in partners:
         pl.semaphore_signal(barrier, inc=1, device_id=partner, device_id_type=MESH)
     for copy in small:
@@ -196,6 +220,11 @@
 
     each(lambda j: relay(j).start())
 
+    @pl.when(core == 1)
+    def _():
+        each(lambda j: pair_down(j).start(), J2)
+
+
     def send_first(j):
         load_gate(j).wait()
         load_up(j).wait()
@@ -254,8 +283,15 @@
             scaled[j], wgu[j, 3], (((1,), (1,)), ((), ())), preferred_element_type=F32
         )
 
+    def ready_down(j):
+        load_down(j).wait()
+
+        @pl.when(core == 1)
+        def _():
+            pair_down(j).wait_recv()
+            core_down(j).start()
+
     def send_down(j):
-        load_down(j).wait()
         d_own(0, j).start()
         d_own(1, j).start()
 
@@ -270,97 +306,145 @@
         d_forward(j).wait_recv()
         d_share(3, j).start()
 
+    low = lax.broadcasted_iota(jnp.int32, (2 * TOK, 128), 1) < 64
+
     def activate(slots):
         inverse = lax.rsqrt(jnp.sum(ssq[...], axis=1, keepdims=True) * (1.0 / D) + 1e-06)
-        low = lax.broadcasted_iota(jnp.int32, (2 * TOK, 128), 1) < 64
         for s in slots:
             base = s * 2 * HS
             gate = acc[:, base:base + 128] * inverse
             mid = acc[:, base + 128:base + 256] * inverse
             up = pltpu.roll(acc[:, base + 256:base + 384] * inverse, 64, 1)
             other = jnp.where(low, pltpu.roll(mid, 64, 1), up)
-            hidden[s, :, 0:128] = (gate / (1.0 + jnp.exp(-gate)) * other).astype(BF16)
-            hidden[s, :, 128:192] = (mid / (1.0 + jnp.exp(-mid)) * up)[:, 0:64].astype(BF16)
+            main = (gate / (1.0 + jnp.exp(-gate)) * other).astype(BF16)
+            tail = mid / (1.0 + jnp.exp(-mid)) * up
+            hidden[s, :, 0:128] = main
+            hidden[s, :, 128:192] = tail[:, 0:64].astype(BF16)
+            packed_out[(0, 1, 2, 4)[s]] = main
+            if s % 2 == 0:
+                tail_two[...] = tail
+            else:
+                packed_out[s + 2] = jnp.where(low, tail_two[...], pltpu.roll(tail, 64, 1)).astype(BF16)
+
+    def unpack():
+        for to, start in ((0, TOK), (TOK, 0)):
+            for s in range(NX):
+                pair_hidden[s, to:to + TOK, 0:128] = packed_in[(0, 1, 2, 4)[s], start:start + TOK]
+            for k in (3, 5):
+                tails = packed_in[k, start:start + TOK].astype(F32)
+                pair_hidden[k - 3, to:to + TOK, 128:192] = tails[:, 0:64].astype(BF16)
+                pair_hidden[k - 2, to:to + TOK, 128:192] = pltpu.roll(tails, 64, 1)[:, 0:64].astype(BF16)
 
     def activate_near(j):
         activate(range(3))
+        exchange(0).start()
         home_inv[...] = jnp.broadcast_to(
             lax.rsqrt(jnp.sum(home_ssq[...], axis=1, keepdims=True) * (1.0 / D) + 1e-06), (TOK, 128)
         )
 
     staged(J, [(0, 0, pick_rows), (1, 0, pass_rows), (0, 0, pass_weights), (2, 0, near_dots)])
     pass_rows(J - 1)
+    each(ready_down, J2)
     send_down(0)
     send_down(1)
     staged(
         J,
         [(0, 0, share_far), (3 - J, J - 2, near_dots), (1, 0, far_dots), (4 - J, J - 1, activate_near)],
     )
+    far_dots(J - 1)
+    activate((3,))
+    exchange(1).start()
     pass_down(0)
     send_down(2)
-    far_dots(J - 1)
-    activate((3,))
-
-    def half_dots(begin, j):
-        total = jnp.dot(hidden[0, begin:begin + TOK, :], wd[j, 0], preferred_element_type=F32)
-        for s in range(1, NX):
-            total = total + jnp.dot(hidden[s, begin:begin + TOK, :], wd[j, s], preferred_element_type=F32)
-        return total
+    pass_down(1)
+    send_down(3)
+    share_down(0)
+
+    @pl.when(core == 0)
+    def _():
+        each(lambda j: core_down(j).wait_recv(), J2)
+
+    exchange(0).wait_recv()
+    exchange(1).wait_recv()
+    unpack()
 
     def second_dots(j):
         for s in (1, 2, 3):
             d_share_in(s, j).wait_recv()
-        pair_out[j] = half_dots(TOK, j).astype(BF16)
-        back_to_pair(j).start()
-        own_part[j] = half_dots(0, j)
-
-    def add_pair(j):
-        back_to_pair(j).wait_recv()
-        home_out[j] = (own_part[j] + pair_in[j].astype(F32)).astype(BF16)
-        for d in (3, 2, 1):
-            go_home(d, j).start()
+        total = jnp.dot(hidden[0], wd[j, 0, 0:HS, :], preferred_element_type=F32)
+        total = total + jnp.dot(pair_hidden[0], wd[j, 0, HS:, :], preferred_element_type=F32)
+        for s in range(1, NX):
+            total = total + jnp.dot(hidden[s], wd[j, s, 0:HS, :], preferred_element_type=F32)
+            total = total + jnp.dot(pair_hidden[s], wd[j, s, HS:, :], preferred_element_type=F32)
+        home_out[j] = total.astype(BF16)
+        for copy in homes(j)[::-1]:
+            copy.start()
         keep_home(j).start()
 
-    def finish(j):
+    def finish(g):
+        value = home_in[g]
+        total = jnp.dot(combine_hi[...], value, preferred_element_type=F32)
+        total = total + jnp.dot(combine_lo[...], value, preferred_element_type=F32)
+        parts = C // C2
+        lanes = pl.ds(pl.multiple_of(g % parts * C2, C2), C2)
+        residual = arrived[g // parts, :, lanes].astype(F32)
+        normed = (residual * home_inv[:, 0:1] * gain[0:1, cols2(0, g)].astype(F32)).astype(BF16)
+        total = residual + zero_w[:, 0:1] * normed.astype(F32) + total
+        out_buf[g] = total.astype(BF16)
+        store_out(g).start()
+
+    def finish_mine(j):
+        g = half * J2 + j
         keep_home(j).wait()
         for d in (1, 2, 3):
-            go_home(d, j).wait_recv()
-        value = home_in[j]
-        total = jnp.dot(combine_hi[...], value, preferred_element_type=F32)
-        total = total + jnp.dot(combine_lo[...], value, preferred_element_type=F32)
-        residual = arrived[j].astype(F32)
-        normed = (residual * home_inv[:, 0:1] * gain[0:1, cols(j)].astype(F32)).astype(BF16)
-        total = residual + zero_w[:, 0:1] * normed.astype(F32) + total
-        out_buf[j] = total.astype(BF16)
-        store_out(j).start()
-
-    pass_down(1)
-    send_down(3)
-    share_down(0)
+            home_arrival(d, g).wait_recv()
+        finish(g)
+
+    def finish_other(j):
+        g = (1 - half) * J2 + j
+        for d in (0, 1, 2, 3):
+            home_arrival(d, g).wait_recv()
+        finish(g)
+
     staged(
-        J + 3,
+        J2 + 2,
         [
             (0, 0, second_dots), (-2, 2, pass_down), (-4, 4, send_down), (-1, 1, share_down),
-            (1, 0, add_pair), (3, 0, finish),
+            (2, 0, finish_mine), (2, 0, finish_other),
         ],
+        J2,
     )
 
     def drain(j):
-        store_out(j).wait()
         relay(j).wait_send()
         for d in (1, 2, 3):
             dispatch(d, j).wait_send()
-            go_home(d, j).wait_send()
         to_pair(j).wait_send()
-        back_to_pair(j).wait_send()
-        for own, forward, share in ((g_own, g_forward, g_share), (d_own, d_forward, d_share)):
-            own(0, j).wait_send()
-            own(1, j).wait_send()
-            forward(j).wait_send()
-            for s in (1, 2, 3):
-                share(s, j).wait_send()
+
+    def drain_ring(own, forward, share, j):
+        own(0, j).wait_send()
+        own(1, j).wait_send()
+        forward(j).wait_send()
+        for s in (1, 2, 3):
+            share(s, j).wait_send()
+
+    def drain_home(j):
+        for copy in homes(j):
+            copy.wait_send()
 
     each(drain)
+    each(lambda j: drain_ring(g_own, g_forward, g_share, j))
+    each(lambda j: drain_ring(d_own, d_forward, d_share, j), J2)
+    exchange(0).wait_send()
+    exchange(1).wait_send()
+
+    @pl.when(core == 1)
+    def _():
+        each(lambda j: pair_down(j).wait_send(), J2)
+        each(lambda j: core_down(j).wait_send(), J2)
+
+    each(drain_home, J2)
+    each(lambda j: store_out(j).wait(), 2 * J2)
 
 
 def local(blocks, norm_gain, w_gate, w_up, w_down, route_ids, route_weights):
@@ -379,28 +463,30 @@
             pltpu.VMEM((J, TOK, C), BF16),
             pltpu.VMEM((J, 2 * TOK, C), BF16),
             pltpu.VMEM((J, NX, 2 * HS, C), BF16),
-            pltpu.VMEM((J, NX, HS, C), BF16),
+            pltpu.VMEM((J2, NX, 2 * HS, C2), BF16),
             pltpu.VMEM((J, 2 * TOK, C), BF16),
             pltpu.VMEM((2 * TOK, NX * 2 * HS), F32),
             pltpu.VMEM((2 * TOK, 128), F32),
             pltpu.VMEM((TOK, 128), F32),
             pltpu.VMEM((NX, 2 * TOK, HS), BF16),
-            pltpu.VMEM((J, TOK, C), F32),
-            pltpu.VMEM((J, TOK, C), BF16),
-            pltpu.VMEM((J, TOK, C), BF16),
-            pltpu.VMEM((J, TOK, C), BF16),
-            pltpu.VMEM((J, TOK, C), BF16),
-            pltpu.VMEM((J, TOK, C), BF16),
+            pltpu.VMEM((NX, 2 * TOK, HS), BF16),
+            pltpu.VMEM((6, 2 * TOK, 128), BF16),
+            pltpu.VMEM((6, 2 * TOK, 128), BF16),
+            pltpu.VMEM((2 * TOK, 128), F32),
+            pltpu.VMEM((J2, 2 * TOK, C2), BF16),
+            pltpu.VMEM((2 * J2, TOK, C2), BF16),
+            pltpu.VMEM((2 * J2, TOK, C2), BF16),
             pltpu.VMEM((TOK, TOK), BF16),
             pltpu.VMEM((TOK, TOK), BF16),
             pltpu.VMEM((TOK, TOK), BF16),
             pltpu.VMEM((TOK, 128), F32),
             pltpu.VMEM((TOK, 128), F32),
-            dma((3,)), dma((5, J)), dma((J,)),
+            dma((3,)), dma((3, J)), dma((2 * J2,)), dma((2 * J2,)),
             dma((J,)), dma((J,)), dma((3, J)), dma((3, J)), dma((J,)), dma((J,)),
             dma((2, J)), dma((2, J)), dma((J,)), dma((J,)), dma((3, J)), dma((3, J)),
-            dma((2, J)), dma((2, J)), dma((J,)), dma((J,)), dma((3, J)), dma((3, J)),
-            dma((J,)), dma((J,)), dma((3, J)), dma((3, J)),
+            dma((2, J2)), dma((2, J2)), dma((J2,)), dma((J2,)), dma((3, J2)), dma((3, J2)),
+            dma((J2,)), dma((J2,)), dma((J2,)), dma((J2,)), dma((2,)), dma((2,)),
+            dma((7, J2)), dma((4, 2 * J2)),
         ],
         compiler_params=pltpu.CompilerParams(
             collective_id=0, has_side_effects=True, vmem_limit_bytes=60 * 1024 * 1024

time: 98.5 us -> 91.6 us (0.930)
  Pallas kernels: 96.3 us -> 89.3 us
    pallas_call x1, Pallas kernels: 96.3 us -> 89.3 us  [local(): pl.pallas_call(kernel, out_shape=jax.ShapeDtypeStruct(blocks.shape, block...]
where the time goes in v4:
time: 91.6 us; the launch traced here: 91.4 us
  Pallas kernels  89.3 us (97%)
  local copies, waits for them, and re-layouts  2.06 us (2%)
    pallas_call x1, Pallas kernels, local(): pl.pallas_call(kernel, out_shape=jax.ShapeDtypeStruct(blocks.shape, block...  89.3 us
    unnamed x1, local copies, waits for them, and re-layouts  2.06 us

profile of v4, /device:TPU:1, one launch (start us, length us, event | category | flops | bytes accessed | tf_op | source)
XLA Modules:
  0.0 91.4 jit_solution(9342165165044823901)
XLA Ops:
  0.0 89.3 %shard_map.73 = bf16[1,128,3072]{2,1,0:T(8,128)(2,1)} custom-call(bf16[1,128,3072]{2,1,0:T(8,128)(2,1)} %blocks.1, bf16[1,3072]{1,0:T(2,128)(2,1)} %gain_in.1, bf16[1,192,3072]{2,1,0:T(8,128)(2,1)} %bitcast.4, bf16[1,192,3072]{2,1,0:T(8,128)(2,1)} %bitcast.5, bf16[1,192,3072]{2,1,0:T(8,128)(2,1)} %w_down.1, s32[1,2,128]{2,1,0:T(2,128)} %bitcast.6, ...), custom_call_target="tpu_custom_call" | custom-call | flops 3623878656 | bytes 6291456 | tf_op jit(solution)/shard_map/pallas_call | solution.py:453
  89.3 2.1 %copy.9 = bf16[1,128,3072]{2,1,0:T(8,128)(2,1)} copy(bf16[1,128,3072]{2,1,0:T(8,128)(2,1)} %shard_map.73) | data formatting | bytes 1572864

commit v5 on v4

--- a/solution.py
+++ b/solution.py
@@ -351,11 +351,11 @@
         J,
         [(0, 0, share_far), (3 - J, J - 2, near_dots), (1, 0, far_dots), (4 - J, J - 1, activate_near)],
     )
+    pass_down(0)
+    send_down(2)
     far_dots(J - 1)
     activate((3,))
     exchange(1).start()
-    pass_down(0)
-    send_down(2)
     pass_down(1)
     send_down(3)
     share_down(0)
@@ -364,9 +364,40 @@
     def _():
         each(lambda j: core_down(j).wait_recv(), J2)
 
+    def drain(j):
+        relay(j).wait_send()
+        for d in (1, 2, 3):
+            dispatch(d, j).wait_send()
+        to_pair(j).wait_send()
+
+    def drain_ring(own, forward, share, j):
+        own(0, j).wait_send()
+        own(1, j).wait_send()
+        forward(j).wait_send()
+        for s in (1, 2, 3):
+            share(s, j).wait_send()
+
+    def drain_home(j):
+        for copy in homes(j):
+            copy.wait_send()
+
+    def drain_second(j):
+        drain_ring(d_own, d_forward, d_share, j)
+        drain_home(j)
+
+    each(drain)
+    each(lambda j: drain_ring(g_own, g_forward, g_share, j))
+
+    @pl.when(core == 1)
+    def _():
+        each(lambda j: pair_down(j).wait_send(), J2)
+        each(lambda j: core_down(j).wait_send(), J2)
+
     exchange(0).wait_recv()
     exchange(1).wait_recv()
     unpack()
+    exchange(0).wait_send()
+    exchange(1).wait_send()
 
     def second_dots(j):
         for s in (1, 2, 3):
@@ -410,40 +441,11 @@
         J2 + 2,
         [
             (0, 0, second_dots), (-2, 2, pass_down), (-4, 4, send_down), (-1, 1, share_down),
-            (2, 0, finish_mine), (2, 0, finish_other),
+            (2, 0, drain_second), (2, 0, finish_mine), (2, 0, finish_other),
         ],
         J2,
     )
 
-    def drain(j):
-        relay(j).wait_send()
-        for d in (1, 2, 3):
-            dispatch(d, j).wait_send()
-        to_pair(j).wait_send()
-
-    def drain_ring(own, forward, share, j):
-        own(0, j).wait_send()
-        own(1, j).wait_send()
-        forward(j).wait_send()
-        for s in (1, 2, 3):
-            share(s, j).wait_send()
-
-    def drain_home(j):
-        for copy in homes(j):
-            copy.wait_send()
-
-    each(drain)
-    each(lambda j: drain_ring(g_own, g_forward, g_share, j))
-    each(lambda j: drain_ring(d_own, d_forward, d_share, j), J2)
-    exchange(0).wait_send()
-    exchange(1).wait_send()
-
-    @pl.when(core == 1)
-    def _():
-        each(lambda j: pair_down(j).wait_send(), J2)
-        each(lambda j: core_down(j).wait_send(), J2)
-
-    each(drain_home, J2)
     each(lambda j: store_out(j).wait(), 2 * J2)
 
 

time: 91.6 us -> 90.2 us (0.985)
  Pallas kernels: 89.3 us -> 88 us
    pallas_call x1, Pallas kernels: 89.3 us -> 88 us  [local(): pl.pallas_call(kernel, out_shape=jax.ShapeDtypeStruct(blocks.shape, block...]
where the time goes in v5:
time: 90.2 us; the launch traced here: 90 us
  Pallas kernels  88 us (98%)
  local copies, waits for them, and re-layouts  2.06 us (2%)
    pallas_call x1, Pallas kernels, local(): pl.pallas_call(kernel, out_shape=jax.ShapeDtypeStruct(blocks.shape, block...  88 us
    unnamed x1, local copies, waits for them, and re-layouts  2.06 us

profile of v5, /device:TPU:1, one launch (start us, length us, event | category | flops | bytes accessed | tf_op | source)
XLA Modules:
  0.0 90.0 jit_solution(1089872834296712305)
XLA Ops:
  0.0 88.0 %shard_map.73 = bf16[1,128,3072]{2,1,0:T(8,128)(2,1)} custom-call(bf16[1,128,3072]{2,1,0:T(8,128)(2,1)} %blocks.1, bf16[1,3072]{1,0:T(2,128)(2,1)} %gain_in.1, bf16[1,192,3072]{2,1,0:T(8,128)(2,1)} %bitcast.4, bf16[1,192,3072]{2,1,0:T(8,128)(2,1)} %bitcast.5, bf16[1,192,3072]{2,1,0:T(8,128)(2,1)} %w_down.1, s32[1,2,128]{2,1,0:T(2,128)} %bitcast.6, ...), custom_call_target="tpu_custom_call" | custom-call | flops 3623878656 | bytes 6291456 | tf_op jit(solution)/shard_map/pallas_call | solution.py:455
  88.0 2.1 %copy.9 = bf16[1,128,3072]{2,1,0:T(8,128)(2,1)} copy(bf16[1,128,3072]{2,1,0:T(8,128)(2,1)} %shard_map.73) | data formatting | bytes 1572864

commit v6 on v5

--- a/solution.py
+++ b/solution.py
@@ -26,7 +26,7 @@
 def kernel(
     blocks, gain_in, w_gate, w_up, w_down, ids_in, weights_in, out,
     gain, ids, weights, arrived, picked, rows, wgu, wd, scaled, acc, ssq, home_ssq,
-    hidden, pair_hidden, packed_out, packed_in, tail_two, home_out, home_in, out_buf,
+    hidden, pair_hidden, packed_out, packed_in, tail_two, home_out, home_in, start, out_buf,
     gather_m, combine_hi, combine_lo, zero_w, home_inv,
     small_sem, load_sem, down_sem, store_sem, relay_s, relay_r, disp_s, disp_r, pair_s, pair_r,
     gx_s, gx_r, gf_s, gf_r, gd_s, gd_r, dx_s, dx_r, df_s, df_r, dd_s, dd_r,
@@ -393,6 +393,14 @@
         each(lambda j: pair_down(j).wait_send(), J2)
         each(lambda j: core_down(j).wait_send(), J2)
 
+    def begin(g):
+        parts = C // C2
+        lanes = pl.ds(pl.multiple_of(g % parts * C2, C2), C2)
+        residual = arrived[g // parts, :, lanes].astype(F32)
+        normed = (residual * home_inv[:, 0:1] * gain[0:1, cols2(0, g)].astype(F32)).astype(BF16)
+        start[g] = residual + zero_w[:, 0:1] * normed.astype(F32)
+
+    each(begin, 2 * J2)
     exchange(0).wait_recv()
     exchange(1).wait_recv()
     unpack()
@@ -416,11 +424,7 @@
         value = home_in[g]
         total = jnp.dot(combine_hi[...], value, preferred_element_type=F32)
         total = total + jnp.dot(combine_lo[...], value, preferred_element_type=F32)
-        parts = C // C2
-        lanes = pl.ds(pl.multiple_of(g % parts * C2, C2), C2)
-        residual = arrived[g // parts, :, lanes].astype(F32)
-        normed = (residual * home_inv[:, 0:1] * gain[0:1, cols2(0, g)].astype(F32)).astype(BF16)
-        total = residual + zero_w[:, 0:1] * normed.astype(F32) + total
+        total = start[g] + total
         out_buf[g] = total.astype(BF16)
         store_out(g).start()
 
@@ -477,6 +481,7 @@
             pltpu.VMEM((2 * TOK, 128), F32),
             pltpu.VMEM((J2, 2 * TOK, C2), BF16),
             pltpu.VMEM((2 * J2, TOK, C2), BF16),
+            pltpu.VMEM((2 * J2, TOK, C2), F32),
             pltpu.VMEM((2 * J2, TOK, C2), BF16),
             pltpu.VMEM((TOK, TOK), BF16),
             pltpu.VMEM((TOK, TOK), BF16),

time: 90.2 us -> 90.3 us (level)
  no operation moved by 1% of the time
where the time goes in v6:
time: 90.3 us; the launch traced here: 90.1 us
  Pallas kernels  88 us (97%)
  local copies, waits for them, and re-layouts  2.06 us (2%)
    pallas_call x1, Pallas kernels, local(): pl.pallas_call(kernel, out_shape=jax.ShapeDtypeStruct(blocks.shape, block...  88 us
    unnamed x1, local copies, waits for them, and re-layouts  2.06 us

profile of v6, /device:TPU:1, one launch (start us, length us, event | category | flops | bytes accessed | tf_op | source)
XLA Modules:
  0.0 90.1 jit_solution(12855134138190090171)
XLA Ops:
  0.0 88.0 %shard_map.73 = bf16[1,128,3072]{2,1,0:T(8,128)(2,1)} custom-call(bf16[1,128,3072]{2,1,0:T(8,128)(2,1)} %blocks.1, bf16[1,3072]{1,0:T(2,128)(2,1)} %gain_in.1, bf16[1,192,3072]{2,1,0:T(8,128)(2,1)} %bitcast.4, bf16[1,192,3072]{2,1,0:T(8,128)(2,1)} %bitcast.5, bf16[1,192,3072]{2,1,0:T(8,128)(2,1)} %w_down.1, s32[1,2,128]{2,1,0:T(2,128)} %bitcast.6, ...), custom_call_target="tpu_custom_call" | custom-call | flops 3623878656 | bytes 6291456 | tf_op jit(solution)/shard_map/pallas_call | solution.py:459
  88.0 2.1 %copy.9 = bf16[1,128,3072]{2,1,0:T(8,128)(2,1)} copy(bf16[1,128,3072]{2,1,0:T(8,128)(2,1)} %shard_map.73) | data formatting | bytes 1572864
